TPU v7x, 32 devices: a whole 2x2x4 slice. The times are simulated.
32 devices in a mesh: groups: 2 (over x), ctx: 16 (over z, y, core).
Axes of the slice: x: 2, y: 2, z: 4, core: 2. Of those that a mesh axis runs over, the one named last changes fastest.
Arguments:
- residual: bfloat16 [2048, 3072], P(('groups', 'ctx')), parts along dimension 0, may hold values from -36 to 36
- queries: bfloat16 [2048, 3072], P(('groups', 'ctx')), parts along dimension 0, may hold values from -112 to 112
- keys: bfloat16 [2048, 512], P(('groups', 'ctx')), parts along dimension 0, may hold values from -4 to 4
- values: bfloat16 [2048, 512], P(('groups', 'ctx')), parts along dimension 0, may hold values from -6 to 6
- block_order: int32 [64], P('groups'), parts along dimension 0, may hold values from 0 to 31, each once
- expert_ids: int32 [2048, 1], P(('groups', 'ctx')), parts along dimension 0, may hold values from 0 to 3; in each aligned block of 64 rows (0 to 63, 64 to 127, ...) at most 18 rows name the same one
- router: bfloat16 [3072, 4], replicated, may hold values from -0.109375 to 0.109375
- w_gate: bfloat16 [16, 3072, 2048], P('ctx'), may hold values from -0.109375 to 0.109375
- w_up: bfloat16 [16, 3072, 2048], P('ctx'), may hold values from -0.109375 to 0.109375
- w_down: bfloat16 [16, 2048, 3072], P('ctx'), may hold values from -0.0625 to 0.0625
Outputs:
- attended: bfloat16 [2048, 3072], P(('groups', 'ctx')), parts along dimension 0
- mixed: bfloat16 [2048, 3072], P(('groups', 'ctx')), parts along dimension 0
There are 2 independent parts, one for each index of `groups`. A program takes and returns all parts, laid end to end along the dimension named above; an argument that names none is the same for every part. Nothing has to cross between parts.
Inputs may be any that keep to these rules, and one draw needn't show every extreme that they name: `expert_ids`: within the 64 rows of one device no expert is named by more than 18 rows, a bound that some block reaches. `block_order`: every half-block of the sequence stands once.
All inputs are finite; a program needn't handle non-finite values.
Results may differ from a plain program's by a relative error of at most 0.0095.
Values may be sent and summed in bfloat16 or wider, within the bound.
A program may use at most 128 MiB of HBM per device.

v0:
```python
import math

import jax
import jax.numpy as jnp
from jax import lax
from jax.sharding import PartitionSpec as P

HEAD_DIM = 128
MOST = 18


def per_device(
    residual, queries, keys, values, block_order, expert_ids, router, w_gate, w_up, w_down
):
    tokens_here = queries.shape[0]
    half_rows = tokens_here // 2
    ctx_count = lax.axis_size("ctx")
    device = lax.axis_index("ctx")
    places = jnp.arange(2 * ctx_count, dtype=jnp.int32)

    def positions(global_rows):
        hit = global_rows[:, None] // half_rows == places[None, :]
        block = jnp.sum(jnp.where(hit, block_order[None, :], 0), axis=1)
        return block * half_rows + global_rows % half_rows

    query_pos = positions(device * tokens_here + jnp.arange(tokens_here, dtype=jnp.int32))
    kv_count = keys.shape[1] // HEAD_DIM
    head_count = queries.shape[1] // HEAD_DIM
    group = head_count // kv_count
    scale = 1.0 / math.sqrt(HEAD_DIM)
    query_heads = queries.reshape(tokens_here, kv_count, group, HEAD_DIM)
    start_state = (
        jnp.full((kv_count, group, tokens_here), -1e30, jnp.float32),
        jnp.zeros((kv_count, group, tokens_here), jnp.float32),
        jnp.zeros((kv_count, group, tokens_here, HEAD_DIM), jnp.float32),
    )
    key_piece = lax.all_gather(keys, "ctx", axis=0, tiled=True)
    value_piece = lax.all_gather(values, "ctx", axis=0, tiled=True)
    count = key_piece.shape[0]
    key_pos = positions(jnp.arange(count, dtype=jnp.int32))
    key_heads = key_piece.reshape(count, kv_count, HEAD_DIM)
    value_heads = value_piece.reshape(count, kv_count, HEAD_DIM)

    def update(state):
        running, total, summed = state
        scores = (
            jnp.einsum("tkgd,skd->kgts", query_heads, key_heads, preferred_element_type=jnp.float32)
            * scale
        )
        keep = (query_pos[:, None] >= key_pos[None, :])[None, None]
        masked = jnp.where(keep, scores, jnp.float32(-1e30))
        newest = jnp.maximum(running, jnp.max(masked, axis=3))
        weights = jnp.where(keep, jnp.exp(masked - newest[..., None]), jnp.float32(0.0))
        total = jnp.sum(weights, axis=3)
        probs = weights.astype(jnp.bfloat16)
        summed = jnp.einsum(
            "kgts,skd->kgtd", probs, value_heads, preferred_element_type=jnp.float32
        )
        return (newest, total, summed)

    needed = jnp.min(key_pos) <= jnp.max(query_pos)
    running, total, summed = lax.cond(needed, update, lambda state: state, start_state)
    attended_heads = summed / total[..., None]
    attended = (
        jnp.transpose(attended_heads, (2, 0, 1, 3))
        .reshape(tokens_here, head_count * HEAD_DIM)
        .astype(jnp.bfloat16)
    )
    stream = residual.astype(jnp.float32) + attended.astype(jnp.float32)
    normed = (stream * lax.rsqrt(jnp.mean(stream * stream, axis=1, keepdims=True) + 1e-05)).astype(
        jnp.bfloat16
    )
    logits = jnp.dot(normed, router, preferred_element_type=jnp.float32)
    expert_count = router.shape[1]
    expert_range = jnp.arange(expert_count, dtype=jnp.int32)
    hits = expert_ids[:, :, None] == expert_range[None, None, :]
    chosen = jnp.sum(jnp.where(hits, logits[:, None, :], jnp.float32(0.0)), axis=2)
    gate = 1.0 / jnp.sum(jnp.exp(logits - chosen), axis=1)
    replicas = ctx_count // expert_count
    topk = expert_ids.shape[1]
    hit_counts = hits.astype(jnp.int32)
    per_expert = jnp.sum(hit_counts, axis=1)
    earlier = jnp.cumsum(per_expert, axis=0) - per_expert
    rank = jnp.sum(hit_counts * earlier[:, None, :], axis=2)
    slot = expert_ids * MOST + rank
    slot_count = expert_count * MOST
    slot_range = jnp.arange(slot_count, dtype=jnp.int32)
    placing = jnp.sum(
        (slot_range[:, None, None] == slot[None, :, :]).astype(jnp.int32), axis=2
    ).astype(jnp.bfloat16)
    lists = jnp.dot(placing, normed, preferred_element_type=jnp.float32).astype(jnp.bfloat16)
    width = normed.shape[1]
    outgoing = jnp.repeat(lists.reshape(expert_count, MOST, width), replicas, axis=0)
    arrived = lax.all_to_all(outgoing, "ctx", split_axis=0, concat_axis=0, tiled=True)
    flat = arrived.reshape(-1, width)
    gated = jnp.dot(flat, w_gate[0], preferred_element_type=jnp.float32)
    upper = jnp.dot(flat, w_up[0], preferred_element_type=jnp.float32)
    hidden = (jax.nn.silu(gated) * upper).astype(jnp.bfloat16)
    produced = (
        jnp.dot(hidden, w_down[0], preferred_element_type=jnp.float32)
        .astype(jnp.bfloat16)
        .reshape(ctx_count, MOST, width)
    )
    returned = lax.all_to_all(produced, "ctx", split_axis=0, concat_axis=0, tiled=True)
    expert_out = jnp.sum(
        returned.reshape(expert_count, replicas, MOST, width).astype(jnp.float32), axis=1
    )
    expert_out = expert_out.reshape(slot_count, width)
    picked = jnp.take(expert_out, slot.reshape(-1), axis=0).reshape(tokens_here, topk, width)
    mixed = picked[:, 0] * gate[:, None]
    return (attended, mixed.astype(jnp.bfloat16))


def solution(mesh):
    return jax.shard_map(
        per_device,
        mesh=mesh,
        in_specs=(
            P(("groups", "ctx"), None),
            P(("groups", "ctx"), None),
            P(("groups", "ctx"), None),
            P(("groups", "ctx"), None),
            P("groups"),
            P(("groups", "ctx"), None),
            P(),
            P("ctx", None, None),
            P("ctx", None, None),
            P("ctx", None, None),
        ),
        out_specs=(P(("groups", "ctx"), None), P(("groups", "ctx"), None)),
        check_vma=False,
    )
```

profile of v0, /device:TPU:13, one launch (start us, length us, event | category | flops | bytes accessed | tf_op | source)
XLA Modules:
  0.0 265.7 jit_solution(16544665903775777691)
XLA Ops:
  7.2 0.0 copy-start
  7.2 0.0 all-gather.3.cloned.1.call-start
  7.2 0.7 all-gather.3.cloned.1.call-update
  7.9 0.0 all-gather.5.cloned.1.call-start
  8.0 0.7 all-gather.5.cloned.1.call-update
  8.7 0.7 select_reduce_fusion.1
  9.4 0.7 select_reduce_fusion
  10.2 0.6 fusion.48
  10.8 0.6 fusion.50
  12.8 2.2 fusion.52
  15.0 0.7 fusion.45
  15.7 32.8 %all-gather.3.cloned.1.call-done = bf16[1024,512]{1,0:T(8,128)(2,1)} async-done(((bf16[64,512]{1,0:T(8,128)(2,1)}), bf16[1024,512]{1,0:T(8,128)(2,1)}) %all-gather.3.cloned.1.call-update) | async-done | bytes 1048592 | tf_op jit(solution)/shard_map/all_gather | solution.py:37
  48.4 39.0 %all-gather.5.cloned.1.call-done = bf16[1024,512]{1,0:T(8,128)(2,1)} async-done(((bf16[64,512]{1,0:T(8,128)(2,1)}), bf16[1024,512]{1,0:T(8,128)(2,1)}) %all-gather.5.cloned.1.call-update) | async-done | bytes 1048592 | tf_op jit(solution)/shard_map/all_gather | solution.py:38
  87.5 0.0 copy-start.3
  87.5 16.1 %conditional.1 = (f32[4,6,64]{2,1,0:T(8,128)S(1)}, f32[4,6,64,128]{3,2,1,0:T(8,128)S(1)}) conditional(s32[]{:T(128)} %convert_element_type.67, () %tuple.16, (s32[64]{0:T(128)S(1)}, s32[1024]{0:T(1024)S(1)}, bf16[1024,512]{1,0:T(8,128)(2,1)}, bf16[64,3072]{1,0:T(8,128)(2,1)}, bf16[1024,512]{1,0:T(8,128)(2,1)}) %tuple.17), branch_computations={%region_4.5_spmd, %region_5.8_spmd} | conditional | flops 825817600 | bytes 46309696 | solution.py:62
  87.5 0.1 broadcast_compare_fusion
  87.6 1.3 reshape.263
  89.0 1.5 reshape.264
  90.4 4.0 %fusion = (f32[4,6,64]{2,1,0:T(8,128)S(1)}, f32[4,1024,64,6]{1,2,3,0:T(8,128)}) fusion(pred[64,1024]{1,0:T(8,128)(4,1)S(1)} %broadcast_compare_fusion, bf16[64,4,6,128]{3,2,1,0:T(8,128)(2,1)S(1)} %reshape.264, bf16[1024,4,128,1]{2,1,0,3:T(4,128)(2,1)S(1)} %bitcast.57), kind=kOutput, calls=%fused_computation.3 | convolution fusion | flops 407370240 | bytes 7804928 | tf_op jit(solution)/shard_map/cond/branch_1_fun/tkgd,skd->kgts/dot_general | solution.py:47
  94.5 0.0 slice-start
  94.5 2.4 reshape.265
  96.8 0.0 slice-start.1
  96.8 4.7 %fusion.3 = f32[4,6,64,128]{3,2,1,0:T(8,128)S(1)} fusion(f32[4,1024,64,6]{1,2,3,0:T(8,128)} %get-tuple-element.31, f32[4,6,64]{2,1,0:T(8,128)S(1)} %broadcast_maximum_fusion, pred[64,1024]{1,0:T(8,128)(4,1)S(1)} %broadcast_compare_fusion, bf16[1024,4,128,1]{2,1,0,3:T(4,128)(2,1)} %bitcast.58), kind=kOutput, calls=%fused_computation.6 | convolution fusion | flops 410517504 | bytes 8198144 | tf_op jit(solution)/shard_map/cond/branch_1_fun/kgts,skd->kgtd/dot_general | solution.py:56
  101.6 0.0 slice-done
  101.6 0.0 slice-done.1
  101.6 2.0 fusion.2
  103.6 0.3 fusion.31
  103.9 0.3 copy.24
  104.2 0.4 convert_element_type.70
  104.6 0.0 copy-done.3
  104.6 0.0 copy-start.1
  104.6 0.2 multiply_reduce_fusion
  104.9 0.3 convolution_convert_fusion
  105.2 0.1 reshape.271
  105.4 0.3 broadcast_in_dim.92
  105.6 57.9 %all_to_all.10 = bf16[16,18,3072]{2,1,0:T(8,128)(2,1)S(1)} all-to-all(bf16[16,18,3072]{2,1,0:T(8,128)(2,1)S(1)} %bitcast.54), channel_id=1, replica_groups=mesh['groups'=2,'ctx'=16] {'ctx'}, dimensions={0} | all-to-all | bytes 3538944 | tf_op jit(solution)/shard_map/all_to_all | solution.py:94
  163.6 1.5 reshape.273
  165.0 0.0 copy-start.2
  165.0 10.5 %fusion.17 = f32[288,2048]{1,0:T(8,128)} fusion(bf16[288,3072]{1,0:T(8,128)(2,1)} %reshape.273, bf16[1,3072,2048]{2,1,0:T(8,128)(2,1)} %param.19), kind=kOutput, calls=%fused_computation.21 | convolution fusion | flops 3623878656 | bytes 16711680 | tf_op jit(solution)/shard_map/dot_general | solution.py:96
  175.5 0.0 copy-done.2
  175.5 17.8 %fusion.19 = bf16[288,3072]{1,0:T(8,128)(2,1)} fusion(bf16[1,2048,3072]{2,1,0:T(8,128)(2,1)} %param.21, bf16[288,3072]{1,0:T(8,128)(2,1)S(1)} %copy-done.2, bf16[1,3072,2048]{2,1,0:T(8,128)(2,1)} %param.20, f32[288,2048]{1,0:T(8,128)} %fusion.17), kind=kOutput, calls=%fused_computation.24 | convolution fusion | flops 7252180992 | bytes 31064064 | tf_op jit(solution)/shard_map/dot_general | solution.py:100
  193.4 0.0 copy-start.4
  193.4 2.9 %reshape.274 = bf16[16,18,3072]{2,1,0:T(8,128)(2,1)} reshape(bf16[288,3072]{1,0:T(8,128)(2,1)} %fusion.19) | data formatting | bytes 3538944 | tf_op jit(solution)/shard_map/reshape | solution.py:102
  196.2 5.1 %all-to-all-start.1 = ((bf16[16,18,3072]{2,1,0:T(8,128)(2,1)}), bf16[16,18,3072]{2,1,0:T(8,128)(2,1)S(1)}, u32[]{:S(2)}, u32[]{:S(2)}) async-start(bf16[16,18,3072]{2,1,0:T(8,128)(2,1)} %reshape.274), calls=%async_computation.1 | async-start | bytes 4718592 | tf_op jit(solution)/shard_map/all_to_all | solution.py:104
  201.3 0.0 copy-done.4
  201.4 0.0 copy-done.1
  201.4 0.0 copy-done
  201.4 0.3 select_reduce_fusion.2
  201.7 52.6 %all-to-all-done.1 = bf16[16,18,3072]{2,1,0:T(8,128)(2,1)S(1)} async-done(((bf16[16,18,3072]{2,1,0:T(8,128)(2,1)}), bf16[16,18,3072]{2,1,0:T(8,128)(2,1)S(1)}, u32[]{:S(2)}, u32[]{:S(2)}) %all-to-all-start.1) | async-done | bytes 1769504 | tf_op jit(solution)/shard_map/all_to_all | solution.py:104
  254.4 1.4 convert_reduce_fusion
  255.8 1.4 reshape.275
  257.2 0.8 gather_fusion
  258.0 0.9 multiply_convert_fusion
  (9 shorter events, 0.1 us)
Async XLA Ops:
  7.2 194.2 %copy-start = (bf16[3072,4]{0,1:T(4,128)(2,1)S(1)}, bf16[3072,4]{0,1:T(4,128)(2,1)}, u32[]{:S(2)}) copy-start(bf16[3072,4]{0,1:T(4,128)(2,1)} %param.18) | copy-start | bytes 73732
  7.2 41.3 %all-gather.3.cloned.1.call-start = ((), (), s32[]{:S(2)}) async-start(), calls=%async_computation.2 | async-start | bytes 1114112 | tf_op jit(solution)/shard_map/all_gather | solution.py:37
  7.9 79.6 %all-gather.5.cloned.1.call-start = ((), (), s32[]{:S(2)}) async-start(), calls=%async_computation.3 | async-start | bytes 1114112 | tf_op jit(solution)/shard_map/all_gather | solution.py:38
  87.5 17.1 %copy-start.3 = (bf16[64,3072]{1,0:T(8,128)(2,1)S(1)}, bf16[64,3072]{1,0:T(8,128)(2,1)}, u32[]{:S(2)}) copy-start(bf16[64,3072]{1,0:T(8,128)(2,1)} %param.12) | copy-start | bytes 1179652
  94.5 7.1 %slice-start = ((s8[6291456]{0:T(1024)(128)(4,1)}), s8[2097152]{0:T(1024)(128)(4,1)S(1)}, s32[]{:S(2)}) async-start(s8[6291456]{0:T(1024)(128)(4,1)} %bitcast.55), calls=%async_computation.4 | async-start | bytes 4194304 | tf_op jit(solution)/shard_map/cond
  96.8 4.7 %slice-start.1 = ((s8[6291456]{0:T(1024)(128)(4,1)}), s8[4194304]{0:T(1024)(128)(4,1)S(1)}, s32[]{:S(2)}) async-start(s8[6291456]{0:T(1024)(128)(4,1)} %bitcast.55), calls=%async_computation.5 | async-start | bytes 8388608 | tf_op jit(solution)/shard_map/cond
  104.6 96.8 %copy-start.1 = (bf16[64,3072]{1,0:T(8,128)(2,1)}, bf16[64,3072]{1,0:T(8,128)(2,1)S(1)}, u32[]{:S(2)}) copy-start(bf16[64,3072]{1,0:T(8,128)(2,1)S(1)} %convert_element_type.70) | copy-start | bytes 1179652
  165.0 10.5 %copy-start.2 = (bf16[288,3072]{1,0:T(8,128)(2,1)S(1)}, bf16[288,3072]{1,0:T(8,128)(2,1)}, u32[]{:S(2)}) copy-start(bf16[288,3072]{1,0:T(8,128)(2,1)} %reshape.273) | copy-start | bytes 5308420
  193.4 8.0 %copy-start.4 = (s32[64,1]{0,1:T(1,128)S(1)}, s32[64,1]{0,1:T(1,128)}, u32[]{:S(2)}) copy-start(s32[64,1]{0,1:T(1,128)} %param.17) | copy-start | bytes 772
  196.2 58.2 %all-to-all-start.1 = ((bf16[16,18,3072]{2,1,0:T(8,128)(2,1)}), bf16[16,18,3072]{2,1,0:T(8,128)(2,1)S(1)}, u32[]{:S(2)}, u32[]{:S(2)}) async-start(bf16[16,18,3072]{2,1,0:T(8,128)(2,1)} %reshape.274), calls=%async_computation.1 | async-start | bytes 4718592 | tf_op jit(solution)/shard_map/all_to_all | solution.py:104
Sparse Core Ops, SparseCore 0:
  10.2 38.2 all-gather.2
  50.6 36.8 all-gather.4
where the time goes:
time: 266 us
  waiting for transfers between devices  126 us (47%)
  blocking collectives  57.9 us (22%)
  matrix products  37.7 us (14%)
  between operations  15.5 us (6%)
  local copies, waits for them, and re-layouts  12.9 us (5%)
  other arithmetic  10.7 us (4%)
  starting transfers between devices  5.2 us (2%)
    all_to_all x1, blocking collectives, per_device(): lax.all_to_all(outgoing, 'ctx', split_axis=0, concat_axis=0, tiled=True)  57.9 us
    all_to_all x1, waiting for transfers between devices, per_device(): lax.all_to_all(produced, 'ctx', split_axis=0, concat_axis=0, tiled=True)  52.6 us
    all_gather x1, waiting for transfers between devices, per_device(): value_piece = lax.all_gather(values, 'ctx', axis=0, tiled=True)  39 us
    all_gather x1, waiting for transfers between devices, per_device(): key_piece = lax.all_gather(keys, 'ctx', axis=0, tiled=True)  32.8 us
    dot_general x1, matrix products, per_device(): jnp.dot(hidden, w_down[0], preferred_element_type=jnp.float32)  17.8 us
    dot_general x1, matrix products, per_device(): gated = jnp.dot(flat, w_gate[0], preferred_element_type=jnp.float32)  10.5 us
  transfers between devices with their start and end apart: 3, of which 3 were waited for; matrix products, arithmetic and copies ran while one was open for 2% of the time, Pallas kernels for 0%

commit v1 on v0

v1 whole, which is shorter than its diff:
```python
import functools
import math

import jax
import jax.numpy as jnp
from jax import lax
from jax.experimental import pallas as pl
from jax.experimental.pallas import tpu as pltpu
from jax.sharding import PartitionSpec as P

HEAD_DIM = 128
MOST = 18
MAIN = 16
EXT = MOST - MAIN
SEGS = MAIN // EXT
CHUNKS = 3
MESH = pl.DeviceIdType.MESH
BF = jnp.bfloat16
F32 = jnp.float32


def dot(a, b):
    return jnp.dot(a, b, preferred_element_type=F32)


def dot_rows(a, b):
    return lax.dot_general(a, b, (((0,), (0,)), ((), ())), preferred_element_type=F32)


def dot_lanes(a, b):
    return lax.dot_general(a, b, (((1,), (1,)), ((), ())), preferred_element_type=F32)


def iota(shape, axis):
    return lax.broadcasted_iota(jnp.int32, shape, axis)


def fold(wide, pieces):
    width = wide.shape[1] // pieces
    return jnp.concatenate([wide[:, j * width : (j + 1) * width] for j in range(pieces)], axis=0)


def unfold(tall, pieces):
    rows = tall.shape[0] // pieces
    return jnp.concatenate([tall[j * rows : (j + 1) * rows] for j in range(pieces)], axis=1)


def kernel(
    count,
    experts,
    residual,
    queries,
    keys,
    values,
    order,
    ids,
    router_t,
    w_gate,
    w_up,
    w_down,
    attended,
    mixed,
    gate_w,
    up_w,
    down_w,
    kv,
    outbox,
    lists,
    gated,
    upper,
    hidden,
    part,
    from_pair,
    to_group,
    from_group,
    total,
    final,
    weight_sem,
    group_sem,
    pair_sem,
    back_pair_sem,
    back_group_sem,
    back_sem,
):
    tokens, width = queries.shape
    kv_width = keys.shape[1]
    kv_heads = kv_width // HEAD_DIM
    group = width // kv_width
    half_rows = tokens // 2
    reps = count // experts
    halves = reps // 2
    chunk = width // CHUNKS
    seg = chunk // SEGS
    rows_main = count * MAIN
    rows_all = rows_main + count * EXT
    hid = hidden.shape[1]

    me = lax.axis_index("ctx")
    e_me = me // reps
    r_me = lax.rem(me, reps)
    side = lax.rem(r_me, 2)
    h_me = r_me // 2

    def device(e, h, s):
        return e * reps + h * 2 + s

    def place(e, h, s):
        return (s * halves + h) * experts + e

    def e_fwd(i):
        return lax.rem(e_me + i, experts)

    def e_back(i):
        return lax.rem(e_me + experts - i, experts)

    def h_fwd(j):
        return lax.rem(h_me + j, halves)

    def h_back(j):
        return lax.rem(h_me + halves - j, halves)

    def target(e, h, s):
        return (lax.axis_index("groups"), device(e, h, s))

    weight_copies = [
        pltpu.make_async_copy(src.at[0], dst, weight_sem.at[n])
        for n, (src, dst) in enumerate(((w_gate, gate_w), (w_up, up_w), (w_down, down_w)))
    ]

    barrier = pltpu.get_barrier_semaphore()
    partners = [target(e_fwd(i), h_me, side) for i in range(1, experts)]
    partners += [target(e_me, h_fwd(j), side) for j in range(1, halves)]
    partners += [target(e_me, h_me, 1 - side)]
    for partner in partners:
        pl.semaphore_signal(barrier, inc=1, device_id=partner, device_id_type=MESH)

    mine = place(e_me, h_me, side)
    own_rows = pl.ds(pl.multiple_of(mine * tokens, tokens), tokens)
    kv[own_rows, :kv_width] = keys[...]
    kv[own_rows, kv_width:] = values[...]
    pl.semaphore_wait(barrier, len(partners))

    def remote(src, dst, sems, at, to):
        return pltpu.make_async_remote_copy(
            src_ref=src,
            dst_ref=dst,
            send_sem=sems.at[(0,) + at],
            recv_sem=sems.at[(1,) + at],
            device_id=to,
            device_id_type=MESH,
        )

    def first(use, block, source, i):
        return remote(source(e_fwd(i)), block(mine), group_sem, (use, 0, i), target(e_fwd(i), h_me, side))

    def first_in(use, block, i):
        ref = block(place(e_back(i), h_me, side))
        return remote(ref, ref, group_sem, (use, 0, i), target(e_back(i), h_me, side))

    def second(use, block, j, i):
        ref = block(place(e_back(i), h_me, side))
        return remote(ref, ref, group_sem, (use, j, i), target(e_me, h_fwd(j), side))

    def second_in(use, block, j, i):
        ref = block(place(e_back(i), h_back(j), side))
        return remote(ref, ref, group_sem, (use, j, i), target(e_me, h_back(j), side))

    def third(use, block, j, i):
        ref = block(place(e_back(i), h_back(j), side))
        return remote(ref, ref, pair_sem, (use, j, i), target(e_me, h_me, 1 - side))

    def third_in(use, block, j, i):
        ref = block(place(e_back(i), h_back(j), 1 - side))
        return remote(ref, ref, pair_sem, (use, j, i), target(e_me, h_me, 1 - side))

    def start_first(use, block, source):
        for i in range(1, experts):
            first(use, block, source, i).start()
        pass_on(use, block, 0)

    def pass_on(use, block, i):
        for j in range(1, halves):
            second(use, block, j, i).start()
        third(use, block, 0, i).start()

    def forward_first(use, block, i):
        first_in(use, block, i).wait_recv()
        pass_on(use, block, i)

    def forward_second(use, block, i):
        for j in range(1, halves):
            second_in(use, block, j, i).wait_recv()
            third(use, block, j, i).start()

    def arrive(use, block):
        for i in range(experts):
            for j in range(halves):
                third_in(use, block, j, i).wait_recv()

    def sent(use, block, source):
        for i in range(1, experts):
            first(use, block, source, i).wait_send()
        for i in range(experts):
            for j in range(1, halves):
                second(use, block, j, i).wait_send()
            for j in range(halves):
                third(use, block, j, i).wait_send()

    def kv_block(p):
        return kv.at[pl.ds(pl.multiple_of(p * tokens, tokens), tokens)]

    def kv_source(e):
        return kv_block(mine)

    start_first(0, kv_block, kv_source)
    for copy in weight_copies:
        copy.start()

    key_count = count * tokens
    column = iota((1, key_count), 1)
    key_pos = lax.rem(column, half_rows)
    key_half = column // half_rows
    for s in range(2):
        for h in range(halves):
            for e in range(experts):
                for b in range(2):
                    start = order[2 * (e * reps + h * 2 + s) + b] * half_rows
                    at = 2 * ((s * halves + h) * experts + e) + b
                    key_pos = key_pos + jnp.where(key_half == at, start, 0)
    together = math.gcd(group, max(1, group * 1024 // key_count))
    row = lax.rem(iota((together * tokens, 1), 0), tokens)
    query_pos = lax.rem(row, half_rows) + half_rows * jnp.where(
        row < half_rows, order[2 * me], order[2 * me + 1]
    )

    for i in range(1, experts):
        forward_first(0, kv_block, i)
        forward_second(0, kv_block, i - 1)
    forward_second(0, kv_block, experts - 1)
    arrive(0, kv_block)

    scale = 1.0 / math.sqrt(HEAD_DIM)

    @pl.loop(0, kv_heads * (group // together))
    def _(step):
        k = step // (group // together)
        lanes = together * HEAD_DIM
        q_lanes = pl.ds(pl.multiple_of(step * lanes, lanes), lanes)
        q = fold(queries[:, q_lanes], together)
        key = kv[:, pl.ds(pl.multiple_of(k * HEAD_DIM, HEAD_DIM), HEAD_DIM)]
        value = kv[:, pl.ds(pl.multiple_of(kv_width + k * HEAD_DIM, HEAD_DIM), HEAD_DIM)]
        scores = jnp.where(query_pos >= key_pos, dot_lanes(q, key) * scale, F32(-1e30))
        weights = jnp.exp(scores - jnp.max(scores, axis=1, keepdims=True))
        total_weight = jnp.sum(weights, axis=1, keepdims=True)
        out = dot(weights.astype(BF), value) / total_weight
        attended[:, q_lanes] = unfold(out, together).astype(BF)

    stream = residual[...].astype(F32) + attended[...].astype(F32)
    normed = (
        stream * lax.rsqrt(jnp.mean(stream * stream, axis=1, keepdims=True) + 1e-05)
    ).astype(BF)
    expert_of = ids[...]
    hits = expert_of == iota((tokens, experts), 1)
    before = (iota((tokens, tokens), 0) > iota((tokens, tokens), 1)).astype(F32).astype(BF)
    earlier = dot(before, hits.astype(F32).astype(BF))
    rank = jnp.sum(jnp.where(hits, earlier, 0.0), axis=1, keepdims=True).astype(jnp.int32)
    slot_rows = experts * MAIN
    slot = iota((tokens, slot_rows), 1)
    put_main = (
        ((slot // MAIN == expert_of) & (lax.rem(slot, MAIN) == rank)).astype(F32).astype(BF)
    )
    tall_slot = iota((SEGS * tokens, slot_rows), 1)
    tall_piece = iota((SEGS * tokens, slot_rows), 0) // tokens
    tall_expert = jnp.concatenate([expert_of] * SEGS, axis=0)
    tall_rank = jnp.concatenate([rank] * SEGS, axis=0)
    put_ext = (
        (
            (tall_slot // MAIN == tall_expert)
            & (lax.rem(tall_slot, MAIN) // SEGS + MAIN == tall_rank)
            & (lax.rem(tall_slot, SEGS) == tall_piece)
        )
        .astype(F32)
        .astype(BF)
    )

    def list_block(c):
        return lambda p: lists.at[c, pl.ds(pl.multiple_of(p * MAIN, MAIN), MAIN)]

    def list_source(c):
        return lambda e: outbox.at[c, pl.ds(pl.multiple_of(e * MAIN, MAIN), MAIN)]

    for c in range(CHUNKS):
        piece = normed[:, c * chunk : (c + 1) * chunk]
        outbox[c, :, :chunk] = dot_rows(put_main, piece).astype(BF)
        outbox[c, :, chunk:] = dot_rows(put_ext, fold(piece, SEGS)).astype(BF)
        lists[c, pl.ds(pl.multiple_of(mine * MAIN, MAIN), MAIN)] = outbox[
            c, pl.ds(pl.multiple_of(e_me * MAIN, MAIN), MAIN)
        ]
        start_first(1 + c, list_block(c), list_source(c))

    logits = dot_lanes(normed, router_t[...])
    chosen = jnp.sum(jnp.where(hits, logits, F32(0.0)), axis=1, keepdims=True)
    gates = 1.0 / jnp.sum(jnp.exp(logits - chosen), axis=1, keepdims=True)

    ext_rows = count * EXT
    ext_row = lax.rem(iota((SEGS * ext_rows, rows_main), 0), ext_rows)
    ext_piece = iota((SEGS * ext_rows, rows_main), 0) // ext_rows
    ext_from = (ext_row // EXT) * MAIN + lax.rem(ext_row, EXT) * SEGS + ext_piece
    pick_ext = (iota((SEGS * ext_rows, rows_main), 1) == ext_from).astype(F32).astype(BF)

    tile = min(256, hid)

    def forward_lists(c):
        for i in range(1, experts):
            forward_first(1 + c, list_block(c), i)

    def forward_lists_on(c):
        for i in range(experts):
            forward_second(1 + c, list_block(c), i)

    def multiply(c):
        arrive(1 + c, list_block(c))
        tail = dot(pick_ext, lists[c, :rows_main, chunk:]).astype(BF)
        lists[c, rows_main:, :chunk] = unfold(tail, SEGS)
        depth = pl.ds(c * chunk, chunk)

        @pl.loop(0, hid // tile)
        def _(t):
            cols = pl.ds(pl.multiple_of(t * tile, tile), tile)
            x = lists[c, :, :chunk]
            g = dot(x, gate_w[depth, cols])
            u = dot(x, up_w[depth, cols])
            if c > 0:
                g = g + gated[:, cols]
                u = u + upper[:, cols]
            if c < CHUNKS - 1:
                gated[:, cols] = g
                upper[:, cols] = u
            else:
                hidden[:, cols] = (g / (1.0 + jnp.exp(-g)) * u).astype(BF)

    forward_lists(0)
    forward_lists_on(0)
    forward_lists(1)
    weight_copies[0].wait()
    weight_copies[1].wait()
    multiply(0)
    forward_lists_on(1)
    forward_lists(2)
    multiply(1)
    forward_lists_on(2)
    multiply(2)
    weight_copies[2].wait()

    half_main = rows_main // 2
    group_rows = experts * MAIN
    other_rows = pl.ds(pl.multiple_of((1 - side) * half_main, half_main), half_main)

    def back_pair(c):
        return remote(
            part.at[c, other_rows],
            from_pair.at[c],
            back_pair_sem,
            (c,),
            target(e_me, h_me, 1 - side),
        )

    def back_group(c, j):
        return remote(
            to_group.at[c, j - 1],
            from_group.at[c, j - 1],
            back_group_sem,
            (c, j),
            target(e_me, h_fwd(j), side),
        )

    def back(c, i):
        return remote(
            total.at[c, pl.ds(pl.multiple_of(e_fwd(i) * MAIN, MAIN), MAIN)],
            final.at[c, pl.ds(pl.multiple_of(e_me * MAIN, MAIN), MAIN)],
            back_sem,
            (c, i),
            target(e_fwd(i), h_me, side),
        )

    def produce(c):
        y = dot(hidden[...], down_w[:, c * chunk : (c + 1) * chunk]).astype(BF)
        part[c, :, :chunk] = y[:rows_main]
        part[c, :, chunk:] = dot_rows(pick_ext, fold(y[rows_main:], SEGS)).astype(BF)
        back_pair(c).start()

    def own_sum(c, h):
        rows_here = pl.ds(
            pl.multiple_of(side * half_main + h * group_rows, group_rows), group_rows
        )
        rows_there = pl.ds(pl.multiple_of(h * group_rows, group_rows), group_rows)
        return part[c, rows_here].astype(F32) + from_pair[c, rows_there].astype(F32)

    def reduce_pair(c):
        back_pair(c).wait_recv()
        for j in range(1, halves):
            to_group[c, j - 1] = own_sum(c, h_fwd(j)).astype(BF)
            back_group(c, j).start()

    def reduce_group(c):
        acc = own_sum(c, h_me)
        for j in range(1, halves):
            back_group(c, j).wait_recv()
            acc = acc + from_group[c, j - 1].astype(F32)
        total[c] = acc.astype(BF)
        for i in range(1, experts):
            back(c, i).start()
        mine_rows = pl.ds(pl.multiple_of(e_me * MAIN, MAIN), MAIN)
        final[c, mine_rows] = total[c, mine_rows]

    def finish(c):
        for i in range(1, experts):
            back(c, i).wait_recv()
        main = dot(put_main, final[c, :, :chunk])
        tail = unfold(dot(put_ext, final[c, :, chunk:]), SEGS)
        mixed[:, c * chunk : (c + 1) * chunk] = (gates * (main + tail)).astype(BF)

    produce(0)
    produce(1)
    reduce_pair(0)
    produce(2)
    reduce_pair(1)
    reduce_group(0)
    reduce_pair(2)
    reduce_group(1)
    reduce_group(2)
    for c in range(CHUNKS):
        finish(c)

    sent(0, kv_block, kv_source)
    for c in range(CHUNKS):
        sent(1 + c, list_block(c), list_source(c))
        back_pair(c).wait_send()
        for j in range(1, halves):
            back_group(c, j).wait_send()
        for i in range(1, experts):
            back(c, i).wait_send()


def per_device(
    residual, queries, keys, values, block_order, expert_ids, router, w_gate, w_up, w_down
):
    count = lax.axis_size("ctx")
    experts = router.shape[1]
    reps = count // experts
    halves = reps // 2
    tokens, width = queries.shape
    kv_width = keys.shape[1]
    hid = w_gate.shape[2]
    chunk = width // CHUNKS
    packed = chunk + chunk // SEGS
    rows_main = count * MAIN
    rows_all = rows_main + count * EXT
    group_rows = experts * MAIN
    vmem = pl.BlockSpec(memory_space=pltpu.VMEM)
    smem = pl.BlockSpec(memory_space=pltpu.SMEM)
    hbm = pl.BlockSpec(memory_space=pl.ANY)
    dma = pltpu.SemaphoreType.DMA
    out = jax.ShapeDtypeStruct((tokens, width), BF)
    return pl.pallas_call(
        functools.partial(kernel, count, experts),
        out_shape=(out, out),
        in_specs=[vmem, vmem, vmem, vmem, smem, vmem, vmem, hbm, hbm, hbm],
        out_specs=(vmem, vmem),
        scratch_shapes=[
            pltpu.VMEM((width, hid), BF),
            pltpu.VMEM((width, hid), BF),
            pltpu.VMEM((hid, width), BF),
            pltpu.VMEM((count * tokens, 2 * kv_width), BF),
            pltpu.VMEM((CHUNKS, group_rows, packed), BF),
            pltpu.VMEM((CHUNKS, rows_all, packed), BF),
            pltpu.VMEM((rows_all, hid), F32),
            pltpu.VMEM((rows_all, hid), F32),
            pltpu.VMEM((rows_all, hid), BF),
            pltpu.VMEM((CHUNKS, rows_main, packed), BF),
            pltpu.VMEM((CHUNKS, rows_main // 2, packed), BF),
            pltpu.VMEM((CHUNKS, halves - 1, group_rows, packed), BF),
            pltpu.VMEM((CHUNKS, halves - 1, group_rows, packed), BF),
            pltpu.VMEM((CHUNKS, group_rows, packed), BF),
            pltpu.VMEM((CHUNKS, group_rows, packed), BF),
            dma((3,)),
            dma((2, 1 + CHUNKS, halves, experts)),
            dma((2, 1 + CHUNKS, halves, experts)),
            dma((2, CHUNKS)),
            dma((2, CHUNKS, halves)),
            dma((2, CHUNKS, experts)),
        ],
        compiler_params=pltpu.CompilerParams(
            collective_id=0, has_side_effects=True, vmem_limit_bytes=62 * 1024 * 1024
        ),
        cost_estimate=pl.CostEstimate(
            flops=6 * rows_all * width * hid,
            bytes_accessed=6 * width * hid,
            transcendentals=tokens * width * count,
        ),
    )(
        residual,
        queries,
        keys,
        values,
        block_order,
        expert_ids,
        router.T,
        w_gate,
        w_up,
        w_down,
    )


def solution(mesh):
    return jax.shard_map(
        per_device,
        mesh=mesh,
        in_specs=(
            P(("groups", "ctx"), None),
            P(("groups", "ctx"), None),
            P(("groups", "ctx"), None),
            P(("groups", "ctx"), None),
            P("groups"),
            P(("groups", "ctx"), None),
            P(),
            P("ctx", None, None),
            P("ctx", None, None),
            P("ctx", None, None),
        ),
        out_specs=(P(("groups", "ctx"), None), P(("groups", "ctx"), None)),
        check_vma=False,
    )
```

time: 266 us -> 83 us (0.31)
  the two profiles are of different devices: /device:TPU:13 before, /device:TPU:0 now
where the time goes in v1:
time: 83 us; the launch traced here: 82.8 us
  Pallas kernels  77.2 us (93%)
  local copies, waits for them, and re-layouts  4.89 us (6%)
    pallas_call x1, Pallas kernels, per_device(): pl.pallas_call(functools.partial(kernel, count, experts), out_shape=(out,...  77.2 us
    unnamed x3, local copies, waits for them, and re-layouts  4.89 us

profile of v1, /device:TPU:0, one launch (start us, length us, event | category | flops | bytes accessed | tf_op | source)
XLA Modules:
  0.0 82.8 jit_solution(10566869266193129594)
XLA Ops:
  0.6 1.4 %copy.12.ids = s32[64,1]{1,0:T(8,128)} copy(s32[64,1]{0,1:T(1,128)} %param.15) | data formatting | bytes 512 | tf_op args[5]
  2.0 77.2 %shard_map.113 = (bf16[64,3072]{1,0:T(8,128)(2,1)}, bf16[64,3072]{1,0:T(8,128)(2,1)}) custom-call(bf16[64,3072]{1,0:T(8,128)(2,1)} %residual.1, bf16[64,3072]{1,0:T(8,128)(2,1)} %queries.1, bf16[64,512]{1,0:T(8,128)(2,1)} %keys.1, bf16[64,512]{1,0:T(8,128)(2,1)} %values.1, s32[32]{0:T(128)} %order.1, s32[64,1]{1,0:T(8,128)} %copy.12.ids, ...), custom_call_target="tpu_custom_call" | custom-call | flops 10871635968 | bytes 37748736 | tf_op jit(solution)/shard_map/pallas_call | solution.py:465
  79.2 1.8 %copy.15 = bf16[64,3072]{1,0:T(8,128)(2,1)} copy(bf16[64,3072]{1,0:T(8,128)(2,1)} %get-tuple-element.4) | data formatting | bytes 786432
  81.0 1.8 %copy.16 = bf16[64,3072]{1,0:T(8,128)(2,1)} copy(bf16[64,3072]{1,0:T(8,128)(2,1)} %get-tuple-element.5) | data formatting | bytes 786432

commit v2 on v1

--- a/solution.py
+++ b/solution.py
@@ -64,6 +64,9 @@
     up_w,
     down_w,
     kv,
+    key_pos,
+    stats,
+    summed,
     outbox,
     lists,
     gated,
@@ -107,11 +110,20 @@
     def place(e, h, s):
         return (s * halves + h) * experts + e
 
+    paired = experts & (experts - 1) == 0
+
+    def e_paired(i):
+        out = e_me
+        for b in range(i.bit_length()):
+            if (i >> b) & 1:
+                out = out + (1 << b) * (1 - 2 * lax.rem(e_me // (1 << b), 2))
+        return out
+
     def e_fwd(i):
-        return lax.rem(e_me + i, experts)
+        return e_paired(i) if paired else lax.rem(e_me + i, experts)
 
     def e_back(i):
-        return lax.rem(e_me + experts - i, experts)
+        return e_paired(i) if paired else lax.rem(e_me + experts - i, experts)
 
     def h_fwd(j):
         return lax.rem(h_me + j, halves)
@@ -134,8 +146,7 @@
     for partner in partners:
         pl.semaphore_signal(barrier, inc=1, device_id=partner, device_id_type=MESH)
 
-    mine = place(e_me, h_me, side)
-    own_rows = pl.ds(pl.multiple_of(mine * tokens, tokens), tokens)
+    own_rows = pl.ds(pl.multiple_of(me * tokens, tokens), tokens)
     kv[own_rows, :kv_width] = keys[...]
     kv[own_rows, kv_width:] = values[...]
     pl.semaphore_wait(barrier, len(partners))
@@ -151,26 +162,26 @@
         )
 
     def first(use, block, source, i):
-        return remote(source(e_fwd(i)), block(mine), group_sem, (use, 0, i), target(e_fwd(i), h_me, side))
+        return remote(source(e_fwd(i)), block(e_me, h_me, side), group_sem, (use, 0, i), target(e_fwd(i), h_me, side))
 
     def first_in(use, block, i):
-        ref = block(place(e_back(i), h_me, side))
+        ref = block(e_back(i), h_me, side)
         return remote(ref, ref, group_sem, (use, 0, i), target(e_back(i), h_me, side))
 
     def second(use, block, j, i):
-        ref = block(place(e_back(i), h_me, side))
+        ref = block(e_back(i), h_me, side)
         return remote(ref, ref, group_sem, (use, j, i), target(e_me, h_fwd(j), side))
 
     def second_in(use, block, j, i):
-        ref = block(place(e_back(i), h_back(j), side))
+        ref = block(e_back(i), h_back(j), side)
         return remote(ref, ref, group_sem, (use, j, i), target(e_me, h_back(j), side))
 
     def third(use, block, j, i):
-        ref = block(place(e_back(i), h_back(j), side))
+        ref = block(e_back(i), h_back(j), side)
         return remote(ref, ref, pair_sem, (use, j, i), target(e_me, h_me, 1 - side))
 
     def third_in(use, block, j, i):
-        ref = block(place(e_back(i), h_back(j), 1 - side))
+        ref = block(e_back(i), h_back(j), 1 - side)
         return remote(ref, ref, pair_sem, (use, j, i), target(e_me, h_me, 1 - side))
 
     def start_first(use, block, source):
@@ -192,10 +203,9 @@
             second_in(use, block, j, i).wait_recv()
             third(use, block, j, i).start()
 
-    def arrive(use, block):
-        for i in range(experts):
-            for j in range(halves):
-                third_in(use, block, j, i).wait_recv()
+    def arrive(use, block, i):
+        for j in range(halves):
+            third_in(use, block, j, i).wait_recv()
 
     def sent(use, block, source):
         for i in range(1, experts):
@@ -206,60 +216,76 @@
             for j in range(halves):
                 third(use, block, j, i).wait_send()
 
-    def kv_block(p):
-        return kv.at[pl.ds(pl.multiple_of(p * tokens, tokens), tokens)]
+    def kv_block(e, h, s):
+        return kv.at[pl.ds(pl.multiple_of(device(e, h, s) * tokens, tokens), tokens)]
 
     def kv_source(e):
-        return kv_block(mine)
+        return kv_block(e_me, h_me, side)
 
     start_first(0, kv_block, kv_source)
     for copy in weight_copies:
         copy.start()
 
-    key_count = count * tokens
-    column = iota((1, key_count), 1)
-    key_pos = lax.rem(column, half_rows)
-    key_half = column // half_rows
-    for s in range(2):
-        for h in range(halves):
-            for e in range(experts):
-                for b in range(2):
-                    start = order[2 * (e * reps + h * 2 + s) + b] * half_rows
-                    at = 2 * ((s * halves + h) * experts + e) + b
-                    key_pos = key_pos + jnp.where(key_half == at, start, 0)
-    together = math.gcd(group, max(1, group * 1024 // key_count))
-    row = lax.rem(iota((together * tokens, 1), 0), tokens)
+    plane = reps * tokens
+    lane = iota((experts, plane), 1)
+    key_half = iota((experts, plane), 0) * (2 * reps) + lane // half_rows
+    positions = lax.rem(lane, half_rows)
+    for at in range(2 * count):
+        positions = positions + jnp.where(key_half == at, order[at] * half_rows, 0)
+    key_pos[...] = positions
+    row = lax.rem(iota((group * tokens, 1), 0), tokens)
     query_pos = lax.rem(row, half_rows) + half_rows * jnp.where(
         row < half_rows, order[2 * me], order[2 * me + 1]
     )
-
-    for i in range(1, experts):
-        forward_first(0, kv_block, i)
-        forward_second(0, kv_block, i - 1)
-    forward_second(0, kv_block, experts - 1)
-    arrive(0, kv_block)
-
     scale = 1.0 / math.sqrt(HEAD_DIM)
 
-    @pl.loop(0, kv_heads * (group // together))
-    def _(step):
-        k = step // (group // together)
-        lanes = together * HEAD_DIM
-        q_lanes = pl.ds(pl.multiple_of(step * lanes, lanes), lanes)
-        q = fold(queries[:, q_lanes], together)
-        key = kv[:, pl.ds(pl.multiple_of(k * HEAD_DIM, HEAD_DIM), HEAD_DIM)]
-        value = kv[:, pl.ds(pl.multiple_of(kv_width + k * HEAD_DIM, HEAD_DIM), HEAD_DIM)]
-        scores = jnp.where(query_pos >= key_pos, dot_lanes(q, key) * scale, F32(-1e30))
-        weights = jnp.exp(scores - jnp.max(scores, axis=1, keepdims=True))
-        total_weight = jnp.sum(weights, axis=1, keepdims=True)
-        out = dot(weights.astype(BF), value) / total_weight
-        attended[:, q_lanes] = unfold(out, together).astype(BF)
-
-    stream = residual[...].astype(F32) + attended[...].astype(F32)
+    def attend(i):
+        e = e_back(i)
+        rows = pl.ds(pl.multiple_of(e * plane, plane), plane)
+        keep = query_pos >= key_pos[pl.ds(e, 1), :]
+
+        @pl.loop(0, kv_heads)
+        def _(step):
+            lanes = group * HEAD_DIM
+            q_lanes = pl.ds(pl.multiple_of(step * lanes, lanes), lanes)
+            q = fold(queries[:, q_lanes], group)
+            key = kv[rows, pl.ds(pl.multiple_of(step * HEAD_DIM, HEAD_DIM), HEAD_DIM)]
+            value = kv[rows, pl.ds(pl.multiple_of(kv_width + step * HEAD_DIM, HEAD_DIM), HEAD_DIM)]
+            scores = jnp.where(keep, dot_lanes(q, key) * scale, F32(-1e30))
+            top = jnp.max(scores, axis=1, keepdims=True)
+            if i > 0:
+                top = jnp.maximum(top, stats[step, :, :1])
+            weights = jnp.exp(scores - top)
+            weight_sum = jnp.sum(weights, axis=1, keepdims=True)
+            out = dot(weights.astype(BF), value)
+            if i > 0:
+                shrink = jnp.exp(stats[step, :, :1] - top)
+                weight_sum = weight_sum + shrink * stats[step, :, 1:]
+                out = out + shrink * summed[step]
+            if i < experts - 1:
+                stats[step, :, :1] = top
+                stats[step, :, 1:] = weight_sum
+                summed[step] = out
+            else:
+                attended[:, q_lanes] = unfold(out / weight_sum, group).astype(BF).astype(F32)
+
+    for i in range(experts):
+        if i + 1 < experts:
+            forward_first(0, kv_block, i + 1)
+        forward_second(0, kv_block, i)
+        if i > 0:
+            arrive(0, kv_block, i - 1)
+            attend(i - 1)
+    arrive(0, kv_block, experts - 1)
+    attend(experts - 1)
+
+    stream = residual[...].astype(F32) + attended[...]
     normed = (
         stream * lax.rsqrt(jnp.mean(stream * stream, axis=1, keepdims=True) + 1e-05)
     ).astype(BF)
-    expert_of = ids[...]
+    ids_here = iota((tokens, tokens), 0) == iota((tokens, tokens), 1)
+    expert_of = jnp.sum(jnp.where(ids_here, ids[...], 0).astype(F32), axis=1, keepdims=True)
+    expert_of = expert_of.astype(jnp.int32)
     hits = expert_of == iota((tokens, experts), 1)
     before = (iota((tokens, tokens), 0) > iota((tokens, tokens), 1)).astype(F32).astype(BF)
     earlier = dot(before, hits.astype(F32).astype(BF))
@@ -284,7 +310,9 @@
     )
 
     def list_block(c):
-        return lambda p: lists.at[c, pl.ds(pl.multiple_of(p * MAIN, MAIN), MAIN)]
+        return lambda e, h, s: lists.at[
+            c, pl.ds(pl.multiple_of(place(e, h, s) * MAIN, MAIN), MAIN)
+        ]
 
     def list_source(c):
         return lambda e: outbox.at[c, pl.ds(pl.multiple_of(e * MAIN, MAIN), MAIN)]
@@ -293,7 +321,7 @@
         piece = normed[:, c * chunk : (c + 1) * chunk]
         outbox[c, :, :chunk] = dot_rows(put_main, piece).astype(BF)
         outbox[c, :, chunk:] = dot_rows(put_ext, fold(piece, SEGS)).astype(BF)
-        lists[c, pl.ds(pl.multiple_of(mine * MAIN, MAIN), MAIN)] = outbox[
+        lists[c, pl.ds(pl.multiple_of(place(e_me, h_me, side) * MAIN, MAIN), MAIN)] = outbox[
             c, pl.ds(pl.multiple_of(e_me * MAIN, MAIN), MAIN)
         ]
         start_first(1 + c, list_block(c), list_source(c))
@@ -319,7 +347,8 @@
             forward_second(1 + c, list_block(c), i)
 
     def multiply(c):
-        arrive(1 + c, list_block(c))
+        for i in range(experts):
+            arrive(1 + c, list_block(c), i)
         tail = dot(pick_ext, lists[c, :rows_main, chunk:]).astype(BF)
         lists[c, rows_main:, :chunk] = unfold(tail, SEGS)
         depth = pl.ds(c * chunk, chunk)
@@ -340,13 +369,13 @@
                 hidden[:, cols] = (g / (1.0 + jnp.exp(-g)) * u).astype(BF)
 
     forward_lists(0)
+    forward_lists(1)
     forward_lists_on(0)
-    forward_lists(1)
+    forward_lists(2)
     weight_copies[0].wait()
     weight_copies[1].wait()
     multiply(0)
     forward_lists_on(1)
-    forward_lists(2)
     multiply(1)
     forward_lists_on(2)
     multiply(2)
@@ -365,14 +394,22 @@
             target(e_me, h_me, 1 - side),
         )
 
-    def back_group(c, j):
+    def block_rows(start, e):
+        return pl.ds(pl.multiple_of(start + e * MAIN, MAIN), MAIN)
+
+    def back_group(c, j, i):
+        rows = block_rows(0, e_fwd(i))
         return remote(
-            to_group.at[c, j - 1],
-            from_group.at[c, j - 1],
+            to_group.at[c, j - 1, rows],
+            from_group.at[c, j - 1, rows],
             back_group_sem,
-            (c, j),
+            (c, j, i),
             target(e_me, h_fwd(j), side),
         )
+
+    def back_group_in(c, j, i):
+        ref = from_group.at[c, j - 1, block_rows(0, e_fwd(i))]
+        return remote(ref, ref, back_group_sem, (c, j, i), target(e_me, h_back(j), side))
 
     def back(c, i):
         return remote(
@@ -389,36 +426,39 @@
         part[c, :, chunk:] = dot_rows(pick_ext, fold(y[rows_main:], SEGS)).astype(BF)
         back_pair(c).start()
 
-    def own_sum(c, h):
-        rows_here = pl.ds(
-            pl.multiple_of(side * half_main + h * group_rows, group_rows), group_rows
-        )
-        rows_there = pl.ds(pl.multiple_of(h * group_rows, group_rows), group_rows)
-        return part[c, rows_here].astype(F32) + from_pair[c, rows_there].astype(F32)
+    turns = list(range(1, experts)) + [0]
+
+    def own_sum(c, h, e):
+        here = part[c, block_rows(side * half_main + h * group_rows, e)]
+        return here.astype(F32) + from_pair[c, block_rows(h * group_rows, e)].astype(F32)
 
     def reduce_pair(c):
         back_pair(c).wait_recv()
-        for j in range(1, halves):
-            to_group[c, j - 1] = own_sum(c, h_fwd(j)).astype(BF)
-            back_group(c, j).start()
+        for i in turns:
+            for j in range(1, halves):
+                e = e_fwd(i)
+                to_group[c, j - 1, block_rows(0, e)] = own_sum(c, h_fwd(j), e).astype(BF)
+                back_group(c, j, i).start()
 
     def reduce_group(c):
-        acc = own_sum(c, h_me)
-        for j in range(1, halves):
-            back_group(c, j).wait_recv()
-            acc = acc + from_group[c, j - 1].astype(F32)
-        total[c] = acc.astype(BF)
-        for i in range(1, experts):
-            back(c, i).start()
-        mine_rows = pl.ds(pl.multiple_of(e_me * MAIN, MAIN), MAIN)
-        final[c, mine_rows] = total[c, mine_rows]
+        for i in turns:
+            e = e_fwd(i)
+            acc = own_sum(c, h_me, e)
+            for j in range(1, halves):
+                back_group_in(c, j, i).wait_recv()
+                acc = acc + from_group[c, j - 1, block_rows(0, e)].astype(F32)
+            if i > 0:
+                total[c, block_rows(0, e)] = acc.astype(BF)
+                back(c, i).start()
+            else:
+                final[c, block_rows(0, e)] = acc.astype(BF)
 
     def finish(c):
         for i in range(1, experts):
             back(c, i).wait_recv()
         main = dot(put_main, final[c, :, :chunk])
         tail = unfold(dot(put_ext, final[c, :, chunk:]), SEGS)
-        mixed[:, c * chunk : (c + 1) * chunk] = (gates * (main + tail)).astype(BF)
+        mixed[:, c * chunk : (c + 1) * chunk] = gates * (main + tail)
 
     produce(0)
     produce(1)
@@ -437,7 +477,8 @@
         sent(1 + c, list_block(c), list_source(c))
         back_pair(c).wait_send()
         for j in range(1, halves):
-            back_group(c, j).wait_send()
+            for i in range(experts):
+                back_group(c, j, i).wait_send()
         for i in range(1, experts):
             back(c, i).wait_send()
 
@@ -452,6 +493,7 @@
     tokens, width = queries.shape
     kv_width = keys.shape[1]
     hid = w_gate.shape[2]
+    group = width // kv_width
     chunk = width // CHUNKS
     packed = chunk + chunk // SEGS
     rows_main = count * MAIN
@@ -461,8 +503,8 @@
     smem = pl.BlockSpec(memory_space=pltpu.SMEM)
     hbm = pl.BlockSpec(memory_space=pl.ANY)
     dma = pltpu.SemaphoreType.DMA
-    out = jax.ShapeDtypeStruct((tokens, width), BF)
-    return pl.pallas_call(
+    out = jax.ShapeDtypeStruct((tokens, width), F32)
+    attended, mixed = pl.pallas_call(
         functools.partial(kernel, count, experts),
         out_shape=(out, out),
         in_specs=[vmem, vmem, vmem, vmem, smem, vmem, vmem, hbm, hbm, hbm],
@@ -472,6 +514,9 @@
             pltpu.VMEM((width, hid), BF),
             pltpu.VMEM((hid, width), BF),
             pltpu.VMEM((count * tokens, 2 * kv_width), BF),
+            pltpu.VMEM((experts, reps * tokens), jnp.int32),
+            pltpu.VMEM((kv_width // HEAD_DIM, group * tokens, 2), F32),
+            pltpu.VMEM((kv_width // HEAD_DIM, group * tokens, HEAD_DIM), F32),
             pltpu.VMEM((CHUNKS, group_rows, packed), BF),
             pltpu.VMEM((CHUNKS, rows_all, packed), BF),
             pltpu.VMEM((rows_all, hid), F32),
@@ -487,7 +532,7 @@
             dma((2, 1 + CHUNKS, halves, experts)),
             dma((2, 1 + CHUNKS, halves, experts)),
             dma((2, CHUNKS)),
-            dma((2, CHUNKS, halves)),
+            dma((2, CHUNKS, halves, experts)),
             dma((2, CHUNKS, experts)),
         ],
         compiler_params=pltpu.CompilerParams(
@@ -504,12 +549,13 @@
         keys,
         values,
         block_order,
-        expert_ids,
+        expert_ids.reshape(1, tokens),
         router.T,
         w_gate,
         w_up,
         w_down,
     )
+    return attended.astype(BF), mixed.astype(BF)
 
 
 def solution(mesh):

time: 83 us -> 85.4 us (1.029)
  local copies, waits for them, and re-layouts: 4.89 us -> 0 us
  other arithmetic: 0 us -> 3.84 us
  Pallas kernels: 77.2 us -> 80.7 us
    unnamed x3 -> x0, local copies, waits for them, and re-layouts: 4.89 us -> none
    convert_element_type x0 -> x2, other arithmetic: none -> 3.84 us  [per_device(): return (attended.astype(BF), mixed.astype(BF))]
    pallas_call x1, Pallas kernels: 77.2 us -> 80.7 us  [per_device(): pl.pallas_call(functools.partial(kernel, count, experts), out_shape=(out,...]
where the time goes in v2:
time: 85.4 us; the launch traced here: 85.2 us
  Pallas kernels  80.7 us (94%)
  other arithmetic  3.84 us (4%)
    pallas_call x1, Pallas kernels, per_device(): pl.pallas_call(functools.partial(kernel, count, experts), out_shape=(out,...  80.7 us
    convert_element_type x2, other arithmetic, per_device(): return (attended.astype(BF), mixed.astype(BF))  3.84 us

profile of v2, /device:TPU:0, one launch (start us, length us, event | category | flops | bytes accessed | tf_op | source)
XLA Modules:
  0.0 85.2 jit_solution(15493809769655367745)
XLA Ops:
  0.6 80.7 %shard_map.113 = (f32[64,3072]{1,0:T(8,128)}, f32[64,3072]{1,0:T(8,128)}) custom-call(bf16[64,3072]{1,0:T(8,128)(2,1)} %residual.1, bf16[64,3072]{1,0:T(8,128)(2,1)} %queries.1, bf16[64,512]{1,0:T(8,128)(2,1)} %keys.1, bf16[64,512]{1,0:T(8,128)(2,1)} %values.1, s32[32]{0:T(128)} %order.1, s32[1,64]{1,0:T(1,128)} %bitcast.3, bf16[4,3072]{1,0:T(4,128)(2,1)} %bitcast.2, ...), custom_call_target="tpu_custom_call" | custom-call | flops 10871635968 | bytes 37748736 | tf_op jit(solution)/shard_map/pallas_call | solution.py:507
  81.3 1.9 %convert_element_type.6 = bf16[64,3072]{1,0:T(8,128)(2,1)} convert(f32[64,3072]{1,0:T(8,128)} %get-tuple-element.4) | non-fusion elementwise | flops 196608 | bytes 1179648 | tf_op jit(solution)/shard_map/convert_element_type | solution.py:558
  83.2 1.9 %convert_element_type.7 = bf16[64,3072]{1,0:T(8,128)(2,1)} convert(f32[64,3072]{1,0:T(8,128)} %get-tuple-element.5) | non-fusion elementwise | flops 196608 | bytes 1179648 | tf_op jit(solution)/shard_map/convert_element_type | solution.py:558

commit v3 on v1

--- a/solution.py
+++ b/solution.py
@@ -259,7 +259,9 @@
     normed = (
         stream * lax.rsqrt(jnp.mean(stream * stream, axis=1, keepdims=True) + 1e-05)
     ).astype(BF)
-    expert_of = ids[...]
+    ids_here = iota((tokens, tokens), 0) == iota((tokens, tokens), 1)
+    expert_of = jnp.sum(jnp.where(ids_here, ids[...], 0).astype(F32), axis=1, keepdims=True)
+    expert_of = expert_of.astype(jnp.int32)
     hits = expert_of == iota((tokens, experts), 1)
     before = (iota((tokens, tokens), 0) > iota((tokens, tokens), 1)).astype(F32).astype(BF)
     earlier = dot(before, hits.astype(F32).astype(BF))
@@ -340,13 +342,13 @@
                 hidden[:, cols] = (g / (1.0 + jnp.exp(-g)) * u).astype(BF)
 
     forward_lists(0)
+    forward_lists(1)
     forward_lists_on(0)
-    forward_lists(1)
+    forward_lists(2)
     weight_copies[0].wait()
     weight_copies[1].wait()
     multiply(0)
     forward_lists_on(1)
-    forward_lists(2)
     multiply(1)
     forward_lists_on(2)
     multiply(2)
@@ -504,7 +506,7 @@
         keys,
         values,
         block_order,
-        expert_ids,
+        expert_ids.reshape(1, tokens),
         router.T,
         w_gate,
         w_up,

time: 83 us -> 82.5 us (level)
  local copies, waits for them, and re-layouts: 4.89 us -> 3.53 us
  Pallas kernels: 77.2 us -> 78.1 us
    unnamed x3 -> x2, local copies, waits for them, and re-layouts: 4.89 us -> 3.53 us
    pallas_call x1, Pallas kernels: 77.2 us -> 78.1 us  [per_device(): pl.pallas_call(functools.partial(kernel, count, experts), out_shape=(out,...]
where the time goes in v3:
time: 82.5 us; the launch traced here: 82.3 us
  Pallas kernels  78.1 us (95%)
  local copies, waits for them, and re-layouts  3.53 us (4%)
    pallas_call x1, Pallas kernels, per_device(): pl.pallas_call(functools.partial(kernel, count, experts), out_shape=(out,...  78.1 us
    unnamed x2, local copies, waits for them, and re-layouts  3.53 us

profile of v3, /device:TPU:0, one launch (start us, length us, event | category | flops | bytes accessed | tf_op | source)
XLA Modules:
  0.0 82.3 jit_solution(17787971687877311338)
XLA Ops:
  0.6 78.1 %shard_map.113 = (bf16[64,3072]{1,0:T(8,128)(2,1)}, bf16[64,3072]{1,0:T(8,128)(2,1)}) custom-call(bf16[64,3072]{1,0:T(8,128)(2,1)} %residual.1, bf16[64,3072]{1,0:T(8,128)(2,1)} %queries.1, bf16[64,512]{1,0:T(8,128)(2,1)} %keys.1, bf16[64,512]{1,0:T(8,128)(2,1)} %values.1, s32[32]{0:T(128)} %order.1, s32[1,64]{1,0:T(1,128)} %bitcast.3, ...), custom_call_target="tpu_custom_call" | custom-call | flops 10871635968 | bytes 37748736 | tf_op jit(solution)/shard_map/pallas_call | solution.py:467
  78.7 1.8 %copy.14 = bf16[64,3072]{1,0:T(8,128)(2,1)} copy(bf16[64,3072]{1,0:T(8,128)(2,1)} %get-tuple-element.4) | data formatting | bytes 786432
  80.5 1.8 %copy.15 = bf16[64,3072]{1,0:T(8,128)(2,1)} copy(bf16[64,3072]{1,0:T(8,128)(2,1)} %get-tuple-element.5) | data formatting | bytes 786432
